TPU v7x, 128 devices: a whole 4x4x4 slice. The times are simulated.
128 devices in a mesh: slab: 16 (over z, y_lo, core), coil: 8 (over y_hi, x).
Axes of the slice: x: 4, y: 4 (y_hi: 2, y_lo: 2; y = y_hi * 2 + y_lo), z: 4, core: 2. Of those that a mesh axis runs over, the one named last changes fastest.
Arguments:
- image: float32 [2, 128, 128, 128], P(None, 'slab'), may hold values from -6 to 6
- cotangent: float32 [2, 128, 128, 128], P(None, 'slab'), may hold values from -6 to 6
- sens: float32 [16, 2, 128, 128, 128], P('coil', None, 'slab'), may hold values from -6 to 6
- mask: int32 [128, 128], replicated, may hold values 0 or 1
- labels: int32 [128, 64, 64], P('slab'), may hold values from 0 to 1
- embed_weight: float32 [8, 96], replicated, may hold values from -2 to 2
- ln_gain: float32 [96], replicated, may hold values from 0.1 to 1.9
- qkv_weight: bfloat16 [96, 288], replicated, may hold values from -8 to 8
- proj_weight: bfloat16 [96, 96], replicated, may hold values from -0.625 to 0.625
- unembed_weight: float32 [96, 8], replicated, may hold values from -0.625 to 0.625
Outputs:
- image_grad: float32 [2, 128, 128, 128], P(None, 'slab')
All inputs are finite; a program needn't handle non-finite values.
Results may differ from a plain program's by a relative error of at most 0.028.
The roundings to bfloat16 on the way count: a program that leaves them out, or rounds other values in their place, can miss the bound.
Values sent between devices are 32-bit elements; how exact they have to be, the bound alone decides.
A program may use at most 64 MiB of HBM per device.

v0:
```python
import functools

import jax
import jax.numpy as jnp
import numpy as np
from jax import lax
from jax.experimental import pallas as pl
from jax.experimental.pallas import tpu as pltpu
from jax.sharding import PartitionSpec as P

MESH = pl.DeviceIdType.MESH
F32 = jnp.float32
BF16 = jnp.bfloat16
HEADS = 3
HEAD = 32
CHANNELS = 96
WINDOWS = 8
TOKENS = 512
GROUPS = 4
CHUNK = 256
EPSILON = 1e-5
STEP_SIZE = 0.5
SCALE = HEAD ** -0.5
PENALTY = 1e9


def dft_tables(length):
    index = np.arange(length)
    angle = (index[:, None] * index[None, :] % length) * (2.0 * np.pi / length)
    cos = np.cos(angle) / np.sqrt(length)
    sin = np.sin(angle) / np.sqrt(length)
    forward = np.block([[cos, sin], [-sin, cos]])
    high = forward.astype(jnp.bfloat16)
    low = (forward - high.astype(np.float64)).astype(jnp.bfloat16)
    return np.stack([high, low, np.ascontiguousarray(high.T), np.ascontiguousarray(low.T)])


def selections():
    select = np.zeros((GROUPS, 8, 32), np.float32)
    for t in range(GROUPS):
        for f in range(8):
            part, px, py = f // 4, f // 2 % 2, f % 2
            select[t, f, part * 16 + px * 8 + 2 * t + py] = 1.0
    wide = np.zeros((3, GROUPS, 8, 192), np.float32)
    for slot, piece in enumerate((0, 0, 0, 1, 1, 2)):
        wide[piece, :, :, 32 * slot : 32 * slot + 32] = select
    return wide, np.ascontiguousarray(select.transpose(0, 2, 1))


def dot(left, right):
    return jnp.dot(left, right, preferred_element_type=F32)


def split2(value):
    high = value.astype(BF16)
    return high, (value - high.astype(F32)).astype(BF16)


def split3(value):
    high = value.astype(BF16)
    rest = value - high.astype(F32)
    middle = rest.astype(BF16)
    return high, middle, (rest - middle.astype(F32)).astype(BF16)


def lane_index(shape):
    return lax.broadcasted_iota(jnp.int32, shape, len(shape) - 1)


def prepare_weights(w):
    wide, narrow = w.wide, w.narrow
    emb = w.embed[...]
    w.pad[...] = jnp.zeros((128, 384), F32)
    w.pad[0:8, 0:CHANNELS] = emb
    w.pad[8:16, 0:CHANNELS] = jnp.broadcast_to(w.gain[...], (8, CHANNELS))
    turned = jnp.transpose(w.pad[:, 0:128])
    w.gain_col[...] = jnp.broadcast_to(turned[0:CHANNELS, 8:9], (CHANNELS, 128))
    emb_t = split3(turned[0:CHANNELS, 0:8])
    un = split3(w.unembed[...])
    emb_pieces = split2(emb)
    for t in range(GROUPS):
        w.to_embed[t] = sum(dot(p.astype(F32), wide[i, t]) for i, p in enumerate(emb_t)).astype(BF16)
        w.to_mixed[t] = sum(dot(p.astype(F32), wide[i, t]) for i, p in enumerate(un)).astype(BF16)
        for i, p in enumerate(emb_pieces):
            w.from_embed[i, t] = dot(narrow[t], p.astype(F32)).astype(BF16)
    w.pad[0:CHANNELS, 0:288] = w.qkv[...].astype(F32)
    for b in range(3):
        w.qkv_t[128 * b : 128 * b + 128, :] = jnp.transpose(w.pad[:, 128 * b : 128 * b + 128]).astype(BF16)


def prepare_fields(col, lab, w):
    rows = col.reshape(2, 2, 128, 128)
    low = lane_index((8, 128)) < 64
    for part in range(2):
        for px in range(2):
            both = jnp.concatenate(
                [rows[arr, part, pl.ds(px, 64, stride=2), :] for arr in range(2)], 0
            )
            w.turn[...] = jnp.transpose(both)
            place = 8 * (part * 2 + px)
            for win in range(WINDOWS):
                first = w.turn[8 * ((2 * win + 1) % 16) : 8 * ((2 * win + 1) % 16) + 8, :]
                second = w.turn[8 * ((2 * win + 2) % 16) : 8 * ((2 * win + 2) % 16) + 8, :]
                w.field[win, 0, place : place + 8, :] = jnp.where(low, first, pltpu.roll(second, 64, 1))
                w.field[win, 1, place : place + 8, :] = jnp.where(low, pltpu.roll(first, 64, 1), second)
    w.pad[:, 0:128] = jnp.zeros((128, 128), F32)
    for z in range(8):
        w.pad[8 * z : 8 * z + 8, 0:64] = lab[z].astype(F32)
    w.turn[...] = jnp.transpose(w.pad[:, 0:128])
    for win in range(WINDOWS):
        tile = w.turn[8 * win : 8 * win + 8, :]
        moved = pltpu.roll(pltpu.roll(tile, 4, 0), 64, 1)
        w.label[win] = jnp.where(low, tile, moved)


def one_window(win, w):
    image6 = split3(w.field[win, 0])
    grad6 = split3(w.field[win, 1])
    order = (0, 1, 2, 0, 1, 0)
    image6 = jnp.concatenate([image6[i] for i in order], 0)
    grad6 = jnp.concatenate([grad6[i] for i in order], 0)
    embedded = jnp.concatenate([dot(w.to_embed[t], image6) for t in range(GROUPS)], 1)
    mixed = jnp.concatenate([dot(w.to_mixed[t], grad6) for t in range(GROUPS)], 1)
    label = w.label[win]
    label = jnp.concatenate([label[t : t + 1, :] for t in range(GROUPS)], 1)

    gain = jnp.concatenate([w.gain_col[...]] * GROUPS, 1)
    mean = jnp.sum(embedded, 0, keepdims=True) * (1.0 / CHANNELS)
    centered = embedded - mean
    variance = jnp.sum(centered * centered, 0, keepdims=True) * (1.0 / CHANNELS)
    inverse = lax.rsqrt(variance + EPSILON)
    unit = centered * inverse
    w.unit[...] = unit
    normed = (unit * gain).astype(BF16)
    projected = dot(w.qkv_t[0:288, :][:, 0:CHANNELS], normed).astype(BF16).astype(F32)
    proj = w.proj[...]
    mixed_high, mixed_low = split2(mixed)
    attended = (dot(proj, mixed_high) + dot(proj, mixed_low)).astype(BF16).astype(F32)
    w.mixed[...] = mixed

    row = lax.broadcasted_iota(jnp.int32, (HEAD, TOKENS), 0)
    zero_f = jnp.zeros((HEAD, TOKENS), F32)
    zero = zero_f.astype(BF16)
    label_key = jnp.where(row == 0, label, jnp.where(row == 1, 1.0 - label, 0.0))
    label_query = jnp.where(row == 0, label - 1.0, jnp.where(row == 1, -label, 0.0)) * PENALTY
    label_query = label_query.astype(BF16)
    lane = lane_index((1, 128))
    only_query = ((lane >= 64) & (lane < 96)).astype(F32)
    only_grad = (lane >= 96).astype(F32)
    lane_scale = jnp.where(lane < 96, SCALE, 1.0).astype(F32)

    for head in range(HEADS):
        at = HEAD * head
        query = projected[at : at + HEAD]
        key = projected[CHANNELS + at : CHANNELS + at + HEAD]
        value = projected[2 * CHANNELS + at : 2 * CHANNELS + at + HEAD]
        grad = attended[at : at + HEAD]
        token = jnp.transpose(jnp.concatenate([key, value, query, grad], 0))
        more = jnp.transpose(jnp.concatenate([key, key, label_key, zero_f], 0))
        token_query = (token * only_query).astype(BF16)
        token_grad = (token * only_grad).astype(BF16)
        token = token.astype(BF16)
        left = jnp.concatenate([token, more.astype(BF16)], 1)
        parts = split3(query * (SCALE * float(np.log2(np.e))))
        right = jnp.concatenate(
            [parts[0], zero, zero, zero, parts[1], parts[2], label_query, zero], 0
        )
        right_value = jnp.concatenate([zero, grad.astype(BF16), zero, zero], 0)
        key16 = key.astype(BF16)
        total = jnp.zeros((TOKENS, 128), F32)
        for chunk in range(TOKENS // CHUNK):
            cut = slice(CHUNK * chunk, CHUNK * chunk + CHUNK)
            scores = dot(left, right[:, cut])
            top = jnp.max(scores, 0, keepdims=True)
            weights = jnp.exp2(scores - top)
            soft = weights * (1.0 / jnp.sum(weights, 0, keepdims=True))
            d_soft = dot(token, right_value[:, cut]).astype(BF16).astype(F32)
            inner = jnp.sum(d_soft * soft, 0, keepdims=True)
            d_scores = (soft * (d_soft - inner)).astype(BF16)
            w.d_proj[at : at + HEAD, cut] = dot(key16, d_scores) * SCALE
            total = total + dot(soft.astype(BF16), token_grad[cut, :]) + dot(d_scores, token_query[cut, :])
        total = jnp.transpose(total * lane_scale)
        w.d_proj[CHANNELS + at : CHANNELS + at + HEAD, :] = total[64:96]
        w.d_proj[2 * CHANNELS + at : 2 * CHANNELS + at + HEAD, :] = total[96:128]

    d_normed = dot(w.qkv[...], w.d_proj[...].astype(BF16)).astype(BF16).astype(F32)
    d_unit = d_normed * gain
    unit = w.unit[...]
    first = jnp.sum(d_unit, 0, keepdims=True) * (1.0 / CHANNELS)
    second = jnp.sum(d_unit * unit, 0, keepdims=True) * (1.0 / CHANNELS)
    d_embedded = inverse * (d_unit - first - unit * second) + w.mixed[...]
    high, low = split2(d_embedded)
    result = jnp.zeros((32, 128), F32)
    for t in range(GROUPS):
        cut = slice(128 * t, 128 * t + 128)
        result += dot(w.from_embed[0, t], high[:, cut])
        result += dot(w.from_embed[0, t], low[:, cut])
        result += dot(w.from_embed[1, t], high[:, cut])
    w.d_field[win] = result


def finish_fields(piece, w):
    rows = piece.reshape(2, 128, 128)
    low = lane_index((8, 128)) < 64
    for px in range(2):
        for win in range(WINDOWS):
            real = w.d_field[win, 8 * px : 8 * px + 8, :]
            imag = w.d_field[win, 16 + 8 * px : 24 + 8 * px, :]
            first = 8 * ((2 * win + 1) % 16)
            second = 8 * ((2 * win + 2) % 16)
            w.turn[first : first + 8, :] = jnp.where(low, real, pltpu.roll(imag, 64, 1))
            w.turn[second : second + 8, :] = jnp.where(low, pltpu.roll(real, 64, 1), imag)
        turned = jnp.transpose(w.turn[...])
        for part in range(2):
            rows[part, pl.ds(px, 64, stride=2), :] = turned[64 * part : 64 * part + 64, :]


def product3(left, right):
    return dot(left[0], right[0]) + dot(left[1], right[0]) + dot(left[0], right[1])


def crossed(value):
    top = jnp.concatenate([value[0:128, 0:128], value[128:256, 0:128]], 1)
    bottom = jnp.concatenate([value[0:128, 128:256], value[128:256, 128:256]], 1)
    return jnp.concatenate([top, bottom], 0)


def one_line(x, sens, cot, w):
    g_real = cot[0, pl.ds(x, 128, stride=8), :]
    g_imag = cot[1, pl.ds(x, 128, stride=8), :]
    s = [[sens[coil, part, pl.ds(x, 128, stride=8), :] for part in range(2)] for coil in range(2)]
    real = [s[k][0] * g_real - s[k][1] * g_imag for k in range(2)]
    imag = [s[k][0] * g_imag + s[k][1] * g_real for k in range(2)]
    value = jnp.concatenate([jnp.concatenate(real, 1), jnp.concatenate(imag, 1)], 0)
    forward = (w.tables[0], w.tables[1])
    backward = (w.tables[2], w.tables[3])
    value = crossed(product3(forward, split2(value)))
    value = product3(split2(value), backward)
    kept = w.mask[...].astype(F32)
    kept = jnp.concatenate([kept, kept], 1)
    value = value * jnp.concatenate([kept, kept], 0)
    value = crossed(product3(split2(value), forward))
    value = product3(backward, split2(value))
    real = [value[0:128, 128 * k : 128 * k + 128] for k in range(2)]
    imag = [value[128:256, 128 * k : 128 * k + 128] for k in range(2)]
    w.partial[x, 0] = sum(s[k][0] * real[k] + s[k][1] * imag[k] for k in range(2))
    w.partial[x, 1] = sum(s[k][0] * imag[k] - s[k][1] * real[k] for k in range(2))


class Refs:
    def __init__(self, **refs):
        self.__dict__.update(refs)


WEIGHTS = ("mask", "embed", "gain", "qkv", "proj", "unembed", "wide", "narrow", "tables")
WORK = dict(
    pad=((128, 384), F32),
    gain_col=((CHANNELS, 128), F32),
    to_embed=((GROUPS, CHANNELS, 192), BF16),
    to_mixed=((GROUPS, CHANNELS, 192), BF16),
    from_embed=((2, GROUPS, 32, CHANNELS), BF16),
    qkv_t=((384, 128), BF16),
    turn=((128, 128), F32),
    field=((WINDOWS, 2, 32, 128), F32),
    label=((WINDOWS, 8, 128), F32),
    unit=((CHANNELS, TOKENS), F32),
    mixed=((CHANNELS, TOKENS), F32),
    d_proj=((288, TOKENS), F32),
    d_field=((WINDOWS, 32, 128), F32),
    partial=((8, 2, 128, 128), F32),
)
SLABS = 16
COILS = 8
RING = 4


def kernel(image, cot, sens, labels, *rest):
    weights = rest[: len(WEIGHTS)]
    out = rest[len(WEIGHTS)]
    scratch = rest[len(WEIGHTS) + 1 :]
    w = Refs(**dict(zip(WEIGHTS, weights)), **dict(zip(WORK, scratch)))
    (col, lab, piece, sens_all, cot_all, coil_sum, swin_in, final, sems) = scratch[len(WORK) :]
    (own_sem, lab_sem, col_sem, cot1_sem, cot2_sem, sens_sem, sum_sem, swin_sem, out_sem, send_sem) = [
        sems.at[i] for i in range(10)
    ]
    s = lax.axis_index("slab")
    c = lax.axis_index("coil")
    xi = lax.rem(c, RING)
    sends = []

    def send(source, target, recv, device):
        copy = pltpu.make_async_remote_copy(
            src_ref=source, dst_ref=target, send_sem=send_sem, recv_sem=recv,
            device_id=device, device_id_type=MESH,
        )
        copy.start()
        sends.append(copy)

    def local(source, target, sem):
        pltpu.make_async_copy(source, target, sem).start()

    def await_bytes(ref, sem):
        pltpu.make_async_copy(ref, ref, sem).wait()

    def span(start, size, step):
        return pl.ds(pl.multiple_of(start, step), size)

    two = pl.ds(2 * xi, 2)
    for d in range(1, SLABS):
        t = lax.rem(s + d, SLABS)
        send(cot.at[:, two, span(8 * t, 8, 8), :], cot_all.at[:, s, xi], cot1_sem, {"slab": t})
    local(cot.at[:, two, span(8 * s, 8, 8), :], cot_all.at[:, s, xi], cot1_sem)
    below = lax.rem(s + SLABS - 1, SLABS)
    for arr, field in enumerate((image, cot)):
        for half in range(2):
            xs = span(lax.rem(16 * c + 8 + 8 * half, 128), 8, 8)
            place = slice(8 * half, 8 * half + 8)
            send(field.at[:, 0:4, xs, :], col.at[arr, :, 4:8, place, :], col_sem, {"slab": below})
            local(field.at[:, 4:8, xs, :], col.at[arr, :, 0:4, place, :], col_sem)
    local(labels.at[:, span(8 * c, 8, 8), :], lab, lab_sem)
    for coil in range(2):
        for d in range(1, SLABS):
            t = lax.rem(s + d, SLABS)
            send(
                sens.at[coil, :, :, span(8 * t, 8, 8), :],
                sens_all.at[coil, :, pl.ds(8 * s, 8)],
                sens_sem,
                {"slab": t},
            )
        local(
            sens.at[coil, :, :, span(8 * s, 8, 8), :], sens_all.at[coil, :, pl.ds(8 * s, 8)], sens_sem
        )
    prepare_weights(w)
    await_bytes(cot_all.at[:, :, 0], cot1_sem)
    for d in range(1, RING):
        t = c - xi + lax.rem(xi + d, RING)
        send(cot_all.at[:, :, xi], cot_all.at[:, :, xi], cot2_sem, {"coil": t})
    await_bytes(col, col_sem)
    await_bytes(lab, lab_sem)
    prepare_fields(col, lab, w)
    lax.fori_loop(0, WINDOWS, lambda win, carry: (one_window(win, w), carry)[1], 0)
    finish_fields(piece, w)

    conditional = []

    def send_or_copy(source, target, recv, slab, coil):
        mine = (slab == s) & (coil == c)
        copy = pltpu.make_async_remote_copy(
            src_ref=source, dst_ref=target, send_sem=send_sem, recv_sem=recv,
            device_id={"slab": slab, "coil": coil}, device_id_type=MESH,
        )

        @pl.when(mine)
        def _():
            local(source, target, recv)

        @pl.when(jnp.logical_not(mine))
        def _():
            copy.start()

        conditional.append((mine, copy))

    for half in range(2):
        to_slab = lax.rem(2 * c + 1 + half, SLABS)
        for upper in range(2):
            to_coil = lax.rem(s + upper, SLABS) // 2
            quarter = (1 + 2 * lax.rem(s, 2)) if not upper else (2 - 2 * lax.rem(s, 2))
            send_or_copy(
                piece.at[:, 4 * upper : 4 * upper + 4, 8 * half : 8 * half + 8, :],
                swin_in.at[:, pl.ds(4 * quarter, 4)],
                swin_sem,
                to_slab,
                to_coil,
            )

    await_bytes(sens_all, sens_sem)
    await_bytes(cot_all.at[:, :, 0:3], cot2_sem)
    sens_rows = sens_all.reshape(2, 2, 1024, 128)
    cot_rows = cot_all.reshape(2, 1024, 128)
    for x in range(8):
        one_line(x, sens_rows, cot_rows, w)
        if x % 4 == 3:
            xs = slice(x - 3, x + 1)
            for d in range(1, COILS):
                t = lax.rem(c + d, COILS)
                send(w.partial.at[xs, :, span(16 * t, 16, 16), :], coil_sum.at[d, xs], sum_sem, {"coil": t})
    await_bytes(coil_sum.at[1:8], sum_sem)
    await_bytes(swin_in, swin_sem)
    final_rows = final.reshape(2, 128, 128)
    for x in range(8):
        for part in range(2):
            total = w.partial[x, part, span(16 * c, 16, 16), :]
            for d in range(1, COILS):
                total = total + coil_sum[d, x, part]
            final_rows[part, pl.ds(x, 16, stride=8), :] = total * -STEP_SIZE
    mine16 = cot_all.reshape(2, 128, 8, 128)
    final[...] = final[...] + mine16[:, pl.ds(16 * c, 16)] + swin_in[...]
    for j in range(2):
        for d in range(COILS):
            t = lax.rem(c + d, COILS)
            source = final.at[:, 8 * j : 8 * j + 8]
            target = out.at[:, :, span(8 * s, 8, 8), :]
            if d:
                send(source, target, out_sem, {"slab": 2 * c + j, "coil": t})
            else:
                send_or_copy(source, target, out_sem, 2 * c + j, c)
    await_bytes(out, out_sem)
    for copy in sends:
        copy.wait_send()
    for mine, copy in conditional:
        @pl.when(jnp.logical_not(mine))
        def _(copy=copy):
            copy.wait_send()


def body(image, cotangent, sens, mask, labels, embed_weight, ln_gain, qkv_weight, proj_weight, unembed_weight):
    wide, narrow = selections()
    whole = pl.BlockSpec(memory_space=pltpu.VMEM)
    anywhere = pl.BlockSpec(memory_space=pl.ANY)
    scratch = [pltpu.VMEM(shape, dtype) for shape, dtype in WORK.values()]
    scratch += [
        pltpu.VMEM((2, 2, 8, 16, 128), F32),
        pltpu.VMEM((8, 8, 64), jnp.int32),
        pltpu.VMEM((2, 8, 16, 128), F32),
        pltpu.VMEM((2, 2, 128, 8, 128), F32),
        pltpu.VMEM((2, 16, 4, 2, 8, 128), F32),
        pltpu.VMEM((8, 8, 2, 16, 128), F32),
        pltpu.VMEM((2, 16, 8, 128), F32),
        pltpu.VMEM((2, 16, 8, 128), F32),
        pltpu.SemaphoreType.DMA((10,)),
    ]
    return pl.pallas_call(
        kernel,
        out_shape=jax.ShapeDtypeStruct(image.shape, F32),
        in_specs=[anywhere] * 4 + [whole] * len(WEIGHTS),
        out_specs=anywhere,
        scratch_shapes=scratch,
        compiler_params=pltpu.CompilerParams(has_side_effects=True, vmem_limit_bytes=48 * 1024 * 1024),
    )(
        image, cotangent, sens, labels, mask, embed_weight, ln_gain.reshape(1, CHANNELS), qkv_weight,
        proj_weight, unembed_weight, jnp.asarray(wide), jnp.asarray(narrow), jnp.asarray(dft_tables(128)),
    )


def solution(mesh):
    placed = (
        P(None, "slab", None, None),
        P(None, "slab", None, None),
        P("coil", None, "slab", None, None),
        P(),
        P("slab", None, None),
        P(),
        P(),
        P(),
        P(),
        P(),
    )
    return jax.shard_map(
        body, mesh=mesh, in_specs=placed, out_specs=P(None, "slab", None, None), check_vma=False
    )
```

profile of v0, /device:TPU:33, one launch (start us, length us, event | category | flops | bytes accessed | tf_op | source)
XLA Modules:
  0.0 101.2 jit_solution(14686356570921876784)
XLA Ops:
  0.0 0.8 copy.14.rest_5_
  0.8 0.0 copy-start
  0.8 1.2 %copy-done = f32[2,8,128,128]{3,2,1,0:T(8,128)S(1)} copy-done((f32[2,8,128,128]{3,2,1,0:T(8,128)S(1)}, f32[2,8,128,128]{3,2,1,0:T(8,128)}, u32[]{:S(2)}) %copy-start) | copy-done | bytes 1048600
  2.0 0.0 copy-start.1
  2.0 1.2 %copy-done.1 = f32[2,8,128,128]{3,2,1,0:T(8,128)S(1)} copy-done((f32[2,8,128,128]{3,2,1,0:T(8,128)S(1)}, f32[2,8,128,128]{3,2,1,0:T(8,128)}, u32[]{:S(2)}) %copy-start.1) | copy-done | bytes 1048600
  3.2 0.0 copy-start.2
  3.2 1.0 %copy-done.2 = bf16[4,256,256]{2,1,0:T(8,128)(2,1)S(1)} copy-done((bf16[4,256,256]{2,1,0:T(8,128)(2,1)S(1)}, bf16[4,256,256]{2,1,0:T(8,128)(2,1)}, u32[]{:S(2)}) %copy-start.2) | copy-done | bytes 524312
  4.3 0.0 copy-start.3
  4.3 0.9 copy-done.3
  5.2 0.0 copy-start.4
  5.2 0.9 copy-done.4
  6.1 0.0 copy-start.5
  6.1 0.9 copy-done.5
  7.0 0.0 copy-start.6
  7.0 0.8 copy-done.6
  7.8 0.0 copy-start.7
  7.8 0.8 copy-done.7
  8.7 0.0 copy-start.8
  8.7 0.7 copy-done.8
  9.4 0.0 copy-start.9
  9.4 0.7 copy-done.9
  10.1 0.7 copy-done.10
  10.8 89.5 %shard_map.127 = f32[2,8,128,128]{3,2,1,0:T(8,128)S(1)} custom-call(f32[2,8,128,128]{3,2,1,0:T(8,128)S(1)} %copy-done, f32[2,8,128,128]{3,2,1,0:T(8,128)S(1)} %copy-done.1, f32[2,2,8,128,128]{4,3,2,1,0:T(8,128)} %sens.1, s32[8,64,64]{2,1,0:T(8,128)S(1)} %copy-done.3, s32[128,128]{1,0:T(8,128)S(1)} %copy-done.6, f32[8,96]{1,0:T(8,128)S(1)} %copy-done.9, ...), custom_call_target="tpu_custom_call" | custom-call | tf_op jit(solution)/shard_map/pallas_call | solution.py:432
  100.3 1.0 copy.16
  (1 shorter events, 0.0 us)
Async XLA Ops:
  0.8 1.2 %copy-start = (f32[2,8,128,128]{3,2,1,0:T(8,128)S(1)}, f32[2,8,128,128]{3,2,1,0:T(8,128)}, u32[]{:S(2)}) copy-start(f32[2,8,128,128]{3,2,1,0:T(8,128)} %image.1) | copy-start | bytes 3145732
  2.0 1.2 %copy-start.1 = (f32[2,8,128,128]{3,2,1,0:T(8,128)S(1)}, f32[2,8,128,128]{3,2,1,0:T(8,128)}, u32[]{:S(2)}) copy-start(f32[2,8,128,128]{3,2,1,0:T(8,128)} %cot.1) | copy-start | bytes 3145732
  3.2 1.0 %copy-start.2 = (bf16[4,256,256]{2,1,0:T(8,128)(2,1)S(1)}, bf16[4,256,256]{2,1,0:T(8,128)(2,1)}, u32[]{:S(2)}) copy-start(bf16[4,256,256]{2,1,0:T(8,128)(2,1)} %constant.8.clone.rest_8_) | copy-start | bytes 1572868
  4.3 0.9 copy-start.3
  5.2 0.9 copy-start.4
  6.1 0.9 copy-start.5
  7.0 0.8 copy-start.6
  7.8 0.8 copy-start.7
  8.7 0.7 copy-start.8
  9.4 0.7 copy-start.9
  10.1 0.7 copy-start.10
where the time goes:
time: 102 us; the launch traced here: 101 us
  Pallas kernels  89.5 us (88%)
  local copies, waits for them, and re-layouts  11.7 us (11%)
    pallas_call x1, Pallas kernels, body(): pl.pallas_call(kernel, out_shape=jax.ShapeDtypeStruct(image.shape, F32),...  89.5 us
    unnamed x24, local copies, waits for them, and re-layouts  11.7 us

commit v1 on v0

--- a/solution.py
+++ b/solution.py
@@ -73,10 +73,11 @@
     w.pad[...] = jnp.zeros((128, 384), F32)
     w.pad[0:8, 0:CHANNELS] = emb
     w.pad[8:16, 0:CHANNELS] = jnp.broadcast_to(w.gain[...], (8, CHANNELS))
+    w.pad[16:24, 0:CHANNELS] = w.unembed[...]
     turned = jnp.transpose(w.pad[:, 0:128])
     w.gain_col[...] = jnp.broadcast_to(turned[0:CHANNELS, 8:9], (CHANNELS, 128))
     emb_t = split3(turned[0:CHANNELS, 0:8])
-    un = split3(w.unembed[...])
+    un = split3(turned[0:CHANNELS, 16:24])
     emb_pieces = split2(emb)
     for t in range(GROUPS):
         w.to_embed[t] = sum(dot(p.astype(F32), wide[i, t]) for i, p in enumerate(emb_t)).astype(BF16)
@@ -252,7 +253,17 @@
         self.__dict__.update(refs)
 
 
-WEIGHTS = ("mask", "embed", "gain", "qkv", "proj", "unembed", "wide", "narrow", "tables")
+WEIGHTS = dict(
+    mask=((128, 128), jnp.int32),
+    embed=((8, CHANNELS), F32),
+    gain=((1, CHANNELS), F32),
+    qkv=((CHANNELS, 288), BF16),
+    proj=((CHANNELS, CHANNELS), BF16),
+    unembed=((8, CHANNELS), F32),
+    wide=((3, GROUPS, 8, 192), F32),
+    narrow=((GROUPS, 32, 8), F32),
+    tables=((4, 256, 256), BF16),
+)
 WORK = dict(
     pad=((128, 384), F32),
     gain_col=((CHANNELS, 128), F32),
@@ -269,6 +280,8 @@
     d_field=((WINDOWS, 32, 128), F32),
     partial=((8, 2, 128, 128), F32),
 )
+EARLY = 5
+VMEM_LIMIT = 60 * 1024 * 1024
 SLABS = 16
 COILS = 8
 RING = 4
@@ -277,9 +290,10 @@
 def kernel(image, cot, sens, labels, *rest):
     weights = rest[: len(WEIGHTS)]
     out = rest[len(WEIGHTS)]
-    scratch = rest[len(WEIGHTS) + 1 :]
-    w = Refs(**dict(zip(WEIGHTS, weights)), **dict(zip(WORK, scratch)))
-    (col, lab, piece, sens_all, cot_all, coil_sum, swin_in, final, sems) = scratch[len(WORK) :]
+    held = rest[len(WEIGHTS) + 1 : 2 * len(WEIGHTS) + 1]
+    scratch = rest[2 * len(WEIGHTS) + 1 :]
+    w = Refs(**dict(zip(WEIGHTS, held)), **dict(zip(WORK, scratch)))
+    (col, lab, piece, sens_all, cot_all, coil_sum, swin_in, final, sems, ready) = scratch[len(WORK) :]
     (own_sem, lab_sem, col_sem, cot1_sem, cot2_sem, sens_sem, sum_sem, swin_sem, out_sem, send_sem) = [
         sems.at[i] for i in range(10)
     ]
@@ -304,6 +318,18 @@
 
     def span(start, size, step):
         return pl.ds(pl.multiple_of(start, step), size)
+
+    barrier = pltpu.get_barrier_semaphore()
+    for d in range(1, SLABS):
+        pl.semaphore_signal(barrier, inc=1, device_id={"slab": lax.rem(s + d, SLABS)}, device_id_type=MESH)
+    for d in range(1, COILS):
+        pl.semaphore_signal(barrier, inc=1, device_id={"coil": lax.rem(c + d, COILS)}, device_id_type=MESH)
+    for source, target in zip(weights, held):
+        local(source, target, own_sem)
+    local(labels.at[:, span(8 * c, 8, 8), :], lab, lab_sem)
+    pl.semaphore_wait(barrier, SLABS + COILS - 2)
+    def windows(first, last):
+        lax.fori_loop(first, last, lambda win, carry: (one_window(win, w), carry)[1], 0)
 
     two = pl.ds(2 * xi, 2)
     for d in range(1, SLABS):
@@ -317,7 +343,6 @@
             place = slice(8 * half, 8 * half + 8)
             send(field.at[:, 0:4, xs, :], col.at[arr, :, 4:8, place, :], col_sem, {"slab": below})
             local(field.at[:, 4:8, xs, :], col.at[arr, :, 0:4, place, :], col_sem)
-    local(labels.at[:, span(8 * c, 8, 8), :], lab, lab_sem)
     for coil in range(2):
         for d in range(1, SLABS):
             t = lax.rem(s + d, SLABS)
@@ -330,6 +355,10 @@
         local(
             sens.at[coil, :, :, span(8 * s, 8, 8), :], sens_all.at[coil, :, pl.ds(8 * s, 8)], sens_sem
         )
+    for d in range(1, SLABS):
+        pl.semaphore_signal(ready, inc=1, device_id={"slab": lax.rem(s + d, SLABS)}, device_id_type=MESH)
+    for target in held:
+        await_bytes(target, own_sem)
     prepare_weights(w)
     await_bytes(cot_all.at[:, :, 0], cot1_sem)
     for d in range(1, RING):
@@ -338,9 +367,21 @@
     await_bytes(col, col_sem)
     await_bytes(lab, lab_sem)
     prepare_fields(col, lab, w)
-    lax.fori_loop(0, WINDOWS, lambda win, carry: (one_window(win, w), carry)[1], 0)
+    windows(0, EARLY)
+    await_bytes(sens_all, sens_sem)
+    await_bytes(cot_all.at[:, :, 0:3], cot2_sem)
+    sens_rows = sens_all.reshape(2, 2, 1024, 128)
+    cot_rows = cot_all.reshape(2, 1024, 128)
+    for x in range(8):
+        one_line(x, sens_rows, cot_rows, w)
+        if x % 4 == 3:
+            xs = slice(x - 3, x + 1)
+            for d in range(1, COILS):
+                t = lax.rem(c + d, COILS)
+                send(w.partial.at[xs, :, span(16 * t, 16, 16), :], coil_sum.at[d, xs], sum_sem, {"coil": t})
+    windows(EARLY, WINDOWS)
     finish_fields(piece, w)
-
+    pl.semaphore_wait(ready, SLABS - 1)
     conditional = []
 
     def send_or_copy(source, target, recv, slab, coil):
@@ -373,17 +414,6 @@
                 to_coil,
             )
 
-    await_bytes(sens_all, sens_sem)
-    await_bytes(cot_all.at[:, :, 0:3], cot2_sem)
-    sens_rows = sens_all.reshape(2, 2, 1024, 128)
-    cot_rows = cot_all.reshape(2, 1024, 128)
-    for x in range(8):
-        one_line(x, sens_rows, cot_rows, w)
-        if x % 4 == 3:
-            xs = slice(x - 3, x + 1)
-            for d in range(1, COILS):
-                t = lax.rem(c + d, COILS)
-                send(w.partial.at[xs, :, span(16 * t, 16, 16), :], coil_sum.at[d, xs], sum_sem, {"coil": t})
     await_bytes(coil_sum.at[1:8], sum_sem)
     await_bytes(swin_in, swin_sem)
     final_rows = final.reshape(2, 128, 128)
@@ -415,9 +445,8 @@
 
 def body(image, cotangent, sens, mask, labels, embed_weight, ln_gain, qkv_weight, proj_weight, unembed_weight):
     wide, narrow = selections()
-    whole = pl.BlockSpec(memory_space=pltpu.VMEM)
     anywhere = pl.BlockSpec(memory_space=pl.ANY)
-    scratch = [pltpu.VMEM(shape, dtype) for shape, dtype in WORK.values()]
+    scratch = [pltpu.VMEM(shape, dtype) for held in (WEIGHTS, WORK) for shape, dtype in held.values()]
     scratch += [
         pltpu.VMEM((2, 2, 8, 16, 128), F32),
         pltpu.VMEM((8, 8, 64), jnp.int32),
@@ -428,17 +457,20 @@
         pltpu.VMEM((2, 16, 8, 128), F32),
         pltpu.VMEM((2, 16, 8, 128), F32),
         pltpu.SemaphoreType.DMA((10,)),
+        pltpu.SemaphoreType.REGULAR,
     ]
     return pl.pallas_call(
         kernel,
         out_shape=jax.ShapeDtypeStruct(image.shape, F32),
-        in_specs=[anywhere] * 4 + [whole] * len(WEIGHTS),
+        in_specs=[anywhere] * (4 + len(WEIGHTS)),
         out_specs=anywhere,
         scratch_shapes=scratch,
-        compiler_params=pltpu.CompilerParams(has_side_effects=True, vmem_limit_bytes=48 * 1024 * 1024),
+        compiler_params=pltpu.CompilerParams(
+            collective_id=0, has_side_effects=True, vmem_limit_bytes=VMEM_LIMIT
+        ),
     )(
         image, cotangent, sens, labels, mask, embed_weight, ln_gain.reshape(1, CHANNELS), qkv_weight,
-        proj_weight, unembed_weight, jnp.asarray(wide), jnp.asarray(narrow), jnp.asarray(dft_tables(128)),
+        proj_weight, unembed_weight.T, jnp.asarray(wide), jnp.asarray(narrow), jnp.asarray(dft_tables(128)),
     )
 
 

time: 102 us -> 84.9 us (0.83)
  the two profiles are of different devices: /device:TPU:33 before, /device:TPU:9 now
where the time goes in v1:
time: 84.9 us; the launch traced here: 84.7 us
  Pallas kernels  82.4 us (97%)
  local copies, waits for them, and re-layouts  2.3 us (3%)
    pallas_call x1, Pallas kernels, body(): pl.pallas_call(kernel, out_shape=jax.ShapeDtypeStruct(image.shape, F32),...  82.4 us
    unnamed x1, local copies, waits for them, and re-layouts  2.3 us

profile of v1, /device:TPU:9, one launch (start us, length us, event | category | flops | bytes accessed | tf_op | source)
XLA Modules:
  0.0 84.7 jit_solution(1365915576537591415)
XLA Ops:
  0.0 82.4 %shard_map.127 = f32[2,8,128,128]{3,2,1,0:T(8,128)} custom-call(f32[2,8,128,128]{3,2,1,0:T(8,128)} %image.1, f32[2,8,128,128]{3,2,1,0:T(8,128)} %cot.1, f32[2,2,8,128,128]{4,3,2,1,0:T(8,128)} %sens.1, s32[8,64,64]{2,1,0:T(8,128)} %labels.1, s32[128,128]{1,0:T(8,128)} %rest_0_.1, f32[8,96]{1,0:T(8,128)} %rest_1_.1, f32[1,96]{1,0:T(1,128)} %bitcast.3, ...), custom_call_target="tpu_custom_call" | custom-call | tf_op jit(solution)/shard_map/pallas_call | solution.py:462
  82.4 2.3 %copy.15 = f32[2,8,128,128]{3,2,1,0:T(8,128)} copy(f32[2,8,128,128]{3,2,1,0:T(8,128)} %shard_map.127) | data formatting | bytes 2097152

commit v2 on v1

--- a/solution.py
+++ b/solution.py
@@ -114,7 +114,7 @@
         w.label[win] = jnp.where(low, tile, moved)
 
 
-def one_window(win, w):
+def one_window(win, w, beside=None):
     image6 = split3(w.field[win, 0])
     grad6 = split3(w.field[win, 1])
     order = (0, 1, 2, 0, 1, 0)
@@ -150,7 +150,7 @@
     only_grad = (lane >= 96).astype(F32)
     lane_scale = jnp.where(lane < 96, SCALE, 1.0).astype(F32)
 
-    for head in range(HEADS):
+    def head_operands(head):
         at = HEAD * head
         query = projected[at : at + HEAD]
         key = projected[CHANNELS + at : CHANNELS + at + HEAD]
@@ -167,22 +167,43 @@
             [parts[0], zero, zero, zero, parts[1], parts[2], label_query, zero], 0
         )
         right_value = jnp.concatenate([zero, grad.astype(BF16), zero, zero], 0)
-        key16 = key.astype(BF16)
-        total = jnp.zeros((TOKENS, 128), F32)
-        for chunk in range(TOKENS // CHUNK):
-            cut = slice(CHUNK * chunk, CHUNK * chunk + CHUNK)
-            scores = dot(left, right[:, cut])
-            top = jnp.max(scores, 0, keepdims=True)
-            weights = jnp.exp2(scores - top)
-            soft = weights * (1.0 / jnp.sum(weights, 0, keepdims=True))
-            d_soft = dot(token, right_value[:, cut]).astype(BF16).astype(F32)
-            inner = jnp.sum(d_soft * soft, 0, keepdims=True)
-            d_scores = (soft * (d_soft - inner)).astype(BF16)
-            w.d_proj[at : at + HEAD, cut] = dot(key16, d_scores) * SCALE
-            total = total + dot(soft.astype(BF16), token_grad[cut, :]) + dot(d_scores, token_query[cut, :])
-        total = jnp.transpose(total * lane_scale)
-        w.d_proj[CHANNELS + at : CHANNELS + at + HEAD, :] = total[64:96]
-        w.d_proj[2 * CHANNELS + at : 2 * CHANNELS + at + HEAD, :] = total[96:128]
+        return left, right, token, right_value, key.astype(BF16), token_grad, token_query
+
+    def products(operands, chunk):
+        left, right, token, right_value = operands[:4]
+        cut = slice(CHUNK * chunk, CHUNK * chunk + CHUNK)
+        scores = dot(left, right[:, cut])
+        return scores, dot(token, right_value[:, cut]).astype(BF16)
+
+    chunks = TOKENS // CHUNK
+    steps = [(head, chunk) for head in range(HEADS) for chunk in range(chunks)]
+    operands = {0: head_operands(0)}
+    ahead = [products(operands[0], 0)]
+    for index, (head, chunk) in enumerate(steps):
+        at = HEAD * head
+        cut = slice(CHUNK * chunk, CHUNK * chunk + CHUNK)
+        scores, d_soft = ahead.pop(0)
+        if beside is not None:
+            beside(index)
+        if index + 1 < len(steps):
+            after, after_chunk = steps[index + 1]
+            if after not in operands:
+                operands[after] = head_operands(after)
+            ahead.append(products(operands[after], after_chunk))
+        key16, token_grad, token_query = operands[head][4:]
+        top = jnp.max(scores, 0, keepdims=True)
+        weights = jnp.exp2(scores - top)
+        soft = weights * (1.0 / jnp.sum(weights, 0, keepdims=True))
+        d_soft = d_soft.astype(F32)
+        inner = jnp.sum(d_soft * soft, 0, keepdims=True)
+        d_scores = (soft * (d_soft - inner)).astype(BF16)
+        w.d_proj[at : at + HEAD, cut] = dot(key16, d_scores) * SCALE
+        part = dot(soft.astype(BF16), token_grad[cut, :]) + dot(d_scores, token_query[cut, :])
+        total = part if chunk == 0 else total + part
+        if chunk == chunks - 1:
+            turned = jnp.transpose(total * lane_scale)
+            w.d_proj[CHANNELS + at : CHANNELS + at + HEAD, :] = turned[64:96]
+            w.d_proj[2 * CHANNELS + at : 2 * CHANNELS + at + HEAD, :] = turned[96:128]
 
     d_normed = dot(w.qkv[...], w.d_proj[...].astype(BF16)).astype(BF16).astype(F32)
     d_unit = d_normed * gain
@@ -220,32 +241,39 @@
     return dot(left[0], right[0]) + dot(left[1], right[0]) + dot(left[0], right[1])
 
 
-def crossed(value):
-    top = jnp.concatenate([value[0:128, 0:128], value[128:256, 0:128]], 1)
-    bottom = jnp.concatenate([value[0:128, 128:256], value[128:256, 128:256]], 1)
-    return jnp.concatenate([top, bottom], 0)
-
-
-def one_line(x, sens, cot, w):
-    g_real = cot[0, pl.ds(x, 128, stride=8), :]
-    g_imag = cot[1, pl.ds(x, 128, stride=8), :]
-    s = [[sens[coil, part, pl.ds(x, 128, stride=8), :] for part in range(2)] for coil in range(2)]
-    real = [s[k][0] * g_real - s[k][1] * g_imag for k in range(2)]
-    imag = [s[k][0] * g_imag + s[k][1] * g_real for k in range(2)]
-    value = jnp.concatenate([jnp.concatenate(real, 1), jnp.concatenate(imag, 1)], 0)
-    forward = (w.tables[0], w.tables[1])
-    backward = (w.tables[2], w.tables[3])
-    value = crossed(product3(forward, split2(value)))
+def turned(value, count):
+    blocks = []
+    for coil in range(count):
+        rows = slice(128 * coil, 128 * coil + 128)
+        blocks.append(
+            jnp.concatenate([jnp.transpose(value[rows, 0:128]), jnp.transpose(value[rows, 128:256])], 1)
+        )
+    return jnp.concatenate(blocks, 0)
+
+
+def some_coils(sens, cot, w):
+    coils = [sens[group, k] for group in range(sens.shape[0]) for k in range(2)]
+    count = len(coils)
+    g_real, g_imag = cot[0], cot[1]
+    real = jnp.concatenate([s[0] * g_real - s[1] * g_imag for s in coils], 0)
+    imag = jnp.concatenate([s[0] * g_imag + s[1] * g_real for s in coils], 0)
+    forward = (w.tables[2], w.tables[3])
+    backward = (w.tables[0], w.tables[1])
+    value = turned(product3(split2(jnp.concatenate([real, imag], 1)), forward), count)
+    value = product3(split2(value), forward)
+    kept = jnp.concatenate([w.kept[...]] * count, 0)
+    value = value * jnp.concatenate([kept, kept], 1)
+    value = turned(product3(split2(value), backward), count)
     value = product3(split2(value), backward)
-    kept = w.mask[...].astype(F32)
-    kept = jnp.concatenate([kept, kept], 1)
-    value = value * jnp.concatenate([kept, kept], 0)
-    value = crossed(product3(split2(value), forward))
-    value = product3(backward, split2(value))
-    real = [value[0:128, 128 * k : 128 * k + 128] for k in range(2)]
-    imag = [value[128:256, 128 * k : 128 * k + 128] for k in range(2)]
-    w.partial[x, 0] = sum(s[k][0] * real[k] + s[k][1] * imag[k] for k in range(2))
-    w.partial[x, 1] = sum(s[k][0] * imag[k] - s[k][1] * real[k] for k in range(2))
+    real = sum(
+        s[0] * value[128 * k : 128 * k + 128, 0:128] + s[1] * value[128 * k : 128 * k + 128, 128:256]
+        for k, s in enumerate(coils)
+    )
+    imag = sum(
+        s[0] * value[128 * k : 128 * k + 128, 128:256] - s[1] * value[128 * k : 128 * k + 128, 0:128]
+        for k, s in enumerate(coils)
+    )
+    return real, imag
 
 
 class Refs:
@@ -278,13 +306,27 @@
     mixed=((CHANNELS, TOKENS), F32),
     d_proj=((288, TOKENS), F32),
     d_field=((WINDOWS, 32, 128), F32),
-    partial=((8, 2, 128, 128), F32),
+    kept=((128, 128), F32),
+    line=((2, 128, 128), F32),
 )
-EARLY = 5
+BUFFERS = (
+    ((2, 2, 8, 16, 128), F32),
+    ((8, 8, 64), jnp.int32),
+    ((2, 8, 16, 128), F32),
+    ((8, 2, 2, 128, 128), F32),
+    ((2, 8, 16, 128), F32),
+    ((2, 128, 128), F32),
+    ((16, 2, 8, 128), F32),
+    ((2, 4, 16, 128), F32),
+    ((2, 8, 16, 128), F32),
+)
+SENDING = 6
+EACH = 3
+STRIDE = 45
 VMEM_LIMIT = 60 * 1024 * 1024
 SLABS = 16
 COILS = 8
-RING = 4
+BATCH = 2
 
 
 def kernel(image, cot, sens, labels, *rest):
@@ -293,13 +335,15 @@
     held = rest[len(WEIGHTS) + 1 : 2 * len(WEIGHTS) + 1]
     scratch = rest[2 * len(WEIGHTS) + 1 :]
     w = Refs(**dict(zip(WEIGHTS, held)), **dict(zip(WORK, scratch)))
-    (col, lab, piece, sens_all, cot_all, coil_sum, swin_in, final, sems, ready) = scratch[len(WORK) :]
-    (own_sem, lab_sem, col_sem, cot1_sem, cot2_sem, sens_sem, sum_sem, swin_sem, out_sem, send_sem) = [
-        sems.at[i] for i in range(10)
+    (col, lab, piece, sens_all, own_cot, cot_all, line_parts, halo, final) = (
+        scratch[len(WORK) : len(WORK) + len(BUFFERS)]
+    )
+    sems, sens_sem, ready = scratch[len(WORK) + len(BUFFERS) :]
+    (own_sem, field_sem, col_sem, cot_sem, line_sem, halo_sem, out_sem, send_sem, sens_send_sem) = [
+        sems.at[i] for i in range(9)
     ]
     s = lax.axis_index("slab")
     c = lax.axis_index("coil")
-    xi = lax.rem(c, RING)
     sends = []
 
     def send(source, target, recv, device):
@@ -324,139 +368,122 @@
         pl.semaphore_signal(barrier, inc=1, device_id={"slab": lax.rem(s + d, SLABS)}, device_id_type=MESH)
     for d in range(1, COILS):
         pl.semaphore_signal(barrier, inc=1, device_id={"coil": lax.rem(c + d, COILS)}, device_id_type=MESH)
+    halves = [span(lax.rem(16 * c + 8 + 8 * half, 128), 8, 8) for half in range(2)]
+    places = [slice(8 * half, 8 * half + 8) for half in range(2)]
+    for xs, place in zip(halves, places):
+        local(cot.at[:, :, xs, :], own_cot.at[:, :, place, :], field_sem)
     for source, target in zip(weights, held):
         local(source, target, own_sem)
-    local(labels.at[:, span(8 * c, 8, 8), :], lab, lab_sem)
+    local(labels.at[:, span(8 * c, 8, 8), :], lab, own_sem)
+    for arr, field in enumerate((image, cot)):
+        for xs, place in zip(halves, places):
+            local(field.at[:, 4:8, xs, :], col.at[arr, :, 0:4, place, :], col_sem)
     pl.semaphore_wait(barrier, SLABS + COILS - 2)
+    for d in range(1, SLABS):
+        pl.semaphore_signal(ready, inc=1, device_id={"slab": lax.rem(s + d, SLABS)}, device_id_type=MESH)
+    mine = pl.ds(pl.multiple_of(8 * s, 8), 8)
+    for d in range(1, SLABS):
+        t = lax.rem(s + d, SLABS)
+        send(cot.at[:, :, lax.rem(16 * c + 8 + t, 128), :], cot_all.at[:, mine, :], cot_sem, {"slab": t})
+    local(cot.at[:, :, lax.rem(16 * c + 8 + s, 128), :], cot_all.at[:, mine, :], cot_sem)
+    below = lax.rem(s + SLABS - 1, SLABS)
+    above = lax.rem(s + 1, SLABS)
+    for arr, field in enumerate((image, cot)):
+        for xs, place in zip(halves, places):
+            send(field.at[:, 0:4, xs, :], col.at[arr, :, 4:8, place, :], col_sem, {"slab": below})
+
+    def send_line(slab, coil):
+        pltpu.make_async_remote_copy(
+            src_ref=sens.at[:, :, :, lax.rem(16 * coil + 8 + slab, 128), :],
+            dst_ref=sens_all.at[c, :, :, mine, :],
+            send_sem=sens_send_sem,
+            recv_sem=sens_sem.at[c],
+            device_id={"slab": slab, "coil": coil},
+            device_id_type=MESH,
+        ).start()
+
+    local(sens.at[:, :, :, lax.rem(16 * c + 8 + s, 128), :], sens_all.at[c, :, :, mine, :], sens_sem.at[c])
+    lax.fori_loop(1, SLABS, lambda d, carry: (send_line(lax.rem(s + d, SLABS), c), carry)[1], 0)
+    pl.semaphore_wait(ready, SLABS - 1)
+
+    others = SLABS * (COILS - 1)
+    share = EACH * HEADS * (TOKENS // CHUNK)
+
+    def send_other(k):
+        d = lax.rem(STRIDE * k + 7, others)
+        send_line(lax.rem(s + lax.rem(d, SLABS), SLABS), lax.rem(c + 1 + d // SLABS, COILS))
+
+    for k in range(others - share * SENDING):
+        send_other(k)
+
+    for target in held:
+        await_bytes(target, own_sem)
+    await_bytes(lab, own_sem)
+    prepare_weights(w)
+    w.kept[...] = jnp.transpose(w.mask[...].astype(F32))
+    await_bytes(col, col_sem)
+    prepare_fields(col, lab, w)
+
     def windows(first, last):
         lax.fori_loop(first, last, lambda win, carry: (one_window(win, w), carry)[1], 0)
 
-    two = pl.ds(2 * xi, 2)
+    def window_and_sends(win, carry):
+        first = others - share * SENDING + share * win
+
+        def beside(step):
+            for k in range(EACH):
+                send_other(first + EACH * step + k)
+
+        one_window(win, w, beside)
+        return carry
+
+    lax.fori_loop(0, SENDING, window_and_sends, 0)
+    await_bytes(cot_all, cot_sem)
+    w.line[...] = jnp.zeros((2, 128, 128), F32)
+    for first in range(0, COILS, BATCH):
+        for group in range(first, first + BATCH):
+            await_bytes(sens_all.at[group], sens_sem.at[group])
+        real, imag = some_coils(sens_all.at[first : first + BATCH], cot_all, w)
+        w.line[0] += real
+        w.line[1] += imag
     for d in range(1, SLABS):
         t = lax.rem(s + d, SLABS)
-        send(cot.at[:, two, span(8 * t, 8, 8), :], cot_all.at[:, s, xi], cot1_sem, {"slab": t})
-    local(cot.at[:, two, span(8 * s, 8, 8), :], cot_all.at[:, s, xi], cot1_sem)
-    below = lax.rem(s + SLABS - 1, SLABS)
-    for arr, field in enumerate((image, cot)):
-        for half in range(2):
-            xs = span(lax.rem(16 * c + 8 + 8 * half, 128), 8, 8)
-            place = slice(8 * half, 8 * half + 8)
-            send(field.at[:, 0:4, xs, :], col.at[arr, :, 4:8, place, :], col_sem, {"slab": below})
-            local(field.at[:, 4:8, xs, :], col.at[arr, :, 0:4, place, :], col_sem)
-    for coil in range(2):
-        for d in range(1, SLABS):
-            t = lax.rem(s + d, SLABS)
-            send(
-                sens.at[coil, :, :, span(8 * t, 8, 8), :],
-                sens_all.at[coil, :, pl.ds(8 * s, 8)],
-                sens_sem,
-                {"slab": t},
-            )
-        local(
-            sens.at[coil, :, :, span(8 * s, 8, 8), :], sens_all.at[coil, :, pl.ds(8 * s, 8)], sens_sem
-        )
-    for d in range(1, SLABS):
-        pl.semaphore_signal(ready, inc=1, device_id={"slab": lax.rem(s + d, SLABS)}, device_id_type=MESH)
-    for target in held:
-        await_bytes(target, own_sem)
-    prepare_weights(w)
-    await_bytes(cot_all.at[:, :, 0], cot1_sem)
-    for d in range(1, RING):
-        t = c - xi + lax.rem(xi + d, RING)
-        send(cot_all.at[:, :, xi], cot_all.at[:, :, xi], cot2_sem, {"coil": t})
-    await_bytes(col, col_sem)
-    await_bytes(lab, lab_sem)
-    prepare_fields(col, lab, w)
-    windows(0, EARLY)
-    await_bytes(sens_all, sens_sem)
-    await_bytes(cot_all.at[:, :, 0:3], cot2_sem)
-    sens_rows = sens_all.reshape(2, 2, 1024, 128)
-    cot_rows = cot_all.reshape(2, 1024, 128)
-    for x in range(8):
-        one_line(x, sens_rows, cot_rows, w)
-        if x % 4 == 3:
-            xs = slice(x - 3, x + 1)
-            for d in range(1, COILS):
-                t = lax.rem(c + d, COILS)
-                send(w.partial.at[xs, :, span(16 * t, 16, 16), :], coil_sum.at[d, xs], sum_sem, {"coil": t})
-    windows(EARLY, WINDOWS)
+        send(w.line.at[:, span(8 * t, 8, 8), :], line_parts.at[s], line_sem, {"slab": t})
+    local(w.line.at[:, mine, :], line_parts.at[s], line_sem)
+    windows(SENDING, WINDOWS)
     finish_fields(piece, w)
-    pl.semaphore_wait(ready, SLABS - 1)
-    conditional = []
-
-    def send_or_copy(source, target, recv, slab, coil):
-        mine = (slab == s) & (coil == c)
-        copy = pltpu.make_async_remote_copy(
-            src_ref=source, dst_ref=target, send_sem=send_sem, recv_sem=recv,
-            device_id={"slab": slab, "coil": coil}, device_id_type=MESH,
-        )
-
-        @pl.when(mine)
-        def _():
-            local(source, target, recv)
-
-        @pl.when(jnp.logical_not(mine))
-        def _():
-            copy.start()
-
-        conditional.append((mine, copy))
-
-    for half in range(2):
-        to_slab = lax.rem(2 * c + 1 + half, SLABS)
-        for upper in range(2):
-            to_coil = lax.rem(s + upper, SLABS) // 2
-            quarter = (1 + 2 * lax.rem(s, 2)) if not upper else (2 - 2 * lax.rem(s, 2))
-            send_or_copy(
-                piece.at[:, 4 * upper : 4 * upper + 4, 8 * half : 8 * half + 8, :],
-                swin_in.at[:, pl.ds(4 * quarter, 4)],
-                swin_sem,
-                to_slab,
-                to_coil,
-            )
-
-    await_bytes(coil_sum.at[1:8], sum_sem)
-    await_bytes(swin_in, swin_sem)
-    final_rows = final.reshape(2, 128, 128)
-    for x in range(8):
-        for part in range(2):
-            total = w.partial[x, part, span(16 * c, 16, 16), :]
-            for d in range(1, COILS):
-                total = total + coil_sum[d, x, part]
-            final_rows[part, pl.ds(x, 16, stride=8), :] = total * -STEP_SIZE
-    mine16 = cot_all.reshape(2, 128, 8, 128)
-    final[...] = final[...] + mine16[:, pl.ds(16 * c, 16)] + swin_in[...]
-    for j in range(2):
-        for d in range(COILS):
-            t = lax.rem(c + d, COILS)
-            source = final.at[:, 8 * j : 8 * j + 8]
-            target = out.at[:, :, span(8 * s, 8, 8), :]
-            if d:
-                send(source, target, out_sem, {"slab": 2 * c + j, "coil": t})
-            else:
-                send_or_copy(source, target, out_sem, 2 * c + j, c)
+    send(piece.at[:, 4:8], halo, halo_sem, {"slab": above})
+    await_bytes(line_parts, line_sem)
+    rows = final.reshape(256, 128)
+    parts = line_parts.reshape(16, 16, 128)
+    for x in range(16):
+        rows[pl.ds(x, 16, stride=16), :] = parts[x] * -STEP_SIZE
+    await_bytes(own_cot, field_sem)
+    final[...] = final[...] + own_cot[...]
+    final[:, 4:8] = final[:, 4:8] + piece[:, 0:4]
+    await_bytes(halo, halo_sem)
+    final[:, 0:4] = final[:, 0:4] + halo[...]
+    for d in range(1, COILS):
+        t = lax.rem(c + d, COILS)
+        for xs, place in zip(halves, places):
+            send(final.at[:, :, place, :], out.at[:, :, xs, :], out_sem, {"coil": t})
+    for xs, place in zip(halves, places):
+        local(final.at[:, :, place, :], out.at[:, :, xs, :], out_sem)
+    await_bytes(sens_all.at[0:7], sens_send_sem)
+    await_bytes(sens_all.at[7, :, :, 0:120, :], sens_send_sem)
     await_bytes(out, out_sem)
     for copy in sends:
         copy.wait_send()
-    for mine, copy in conditional:
-        @pl.when(jnp.logical_not(mine))
-        def _(copy=copy):
-            copy.wait_send()
 
 
 def body(image, cotangent, sens, mask, labels, embed_weight, ln_gain, qkv_weight, proj_weight, unembed_weight):
     wide, narrow = selections()
     anywhere = pl.BlockSpec(memory_space=pl.ANY)
     scratch = [pltpu.VMEM(shape, dtype) for held in (WEIGHTS, WORK) for shape, dtype in held.values()]
+    scratch += [pltpu.VMEM(shape, dtype) for shape, dtype in BUFFERS]
     scratch += [
-        pltpu.VMEM((2, 2, 8, 16, 128), F32),
-        pltpu.VMEM((8, 8, 64), jnp.int32),
-        pltpu.VMEM((2, 8, 16, 128), F32),
-        pltpu.VMEM((2, 2, 128, 8, 128), F32),
-        pltpu.VMEM((2, 16, 4, 2, 8, 128), F32),
-        pltpu.VMEM((8, 8, 2, 16, 128), F32),
-        pltpu.VMEM((2, 16, 8, 128), F32),
-        pltpu.VMEM((2, 16, 8, 128), F32),
-        pltpu.SemaphoreType.DMA((10,)),
+        pltpu.SemaphoreType.DMA((9,)),
+        pltpu.SemaphoreType.DMA((COILS,)),
         pltpu.SemaphoreType.REGULAR,
     ]
     return pl.pallas_call(

time: 84.9 us -> 79.6 us (0.938)
  the two profiles are of different devices: /device:TPU:9 before, /device:TPU:38 now
where the time goes in v2:
time: 79.6 us; the launch traced here: 79.4 us
  Pallas kernels  77.1 us (97%)
  local copies, waits for them, and re-layouts  2.3 us (3%)
    pallas_call x1, Pallas kernels, body(): pl.pallas_call(kernel, out_shape=jax.ShapeDtypeStruct(image.shape, F32),...  77.1 us
    unnamed x1, local copies, waits for them, and re-layouts  2.3 us

profile of v2, /device:TPU:38, one launch (start us, length us, event | category | flops | bytes accessed | tf_op | source)
XLA Modules:
  0.0 79.4 jit_solution(14892734924803778160)
XLA Ops:
  0.0 77.1 %shard_map.127 = f32[2,8,128,128]{3,2,1,0:T(8,128)} custom-call(f32[2,8,128,128]{3,2,1,0:T(8,128)} %image.1, f32[2,8,128,128]{3,2,1,0:T(8,128)} %cot.1, f32[2,2,8,128,128]{4,3,2,1,0:T(8,128)} %sens.1, s32[8,64,64]{2,1,0:T(8,128)} %labels.1, s32[128,128]{1,0:T(8,128)} %rest_0_.1, f32[8,96]{1,0:T(8,128)} %rest_1_.1, f32[1,96]{1,0:T(1,128)} %bitcast.3, ...), custom_call_target="tpu_custom_call" | custom-call | tf_op jit(solution)/shard_map/pallas_call | solution.py:489
  77.2 2.3 %copy.15 = f32[2,8,128,128]{3,2,1,0:T(8,128)} copy(f32[2,8,128,128]{3,2,1,0:T(8,128)} %shard_map.127) | data formatting | bytes 2097152

commit v3 on v2

--- a/solution.py
+++ b/solution.py
@@ -319,14 +319,16 @@
     ((16, 2, 8, 128), F32),
     ((2, 4, 16, 128), F32),
     ((2, 8, 16, 128), F32),
+    ((2, 8, 128, 128), F32),
 )
-SENDING = 6
+SENDING = 7
 EACH = 3
 STRIDE = 45
 VMEM_LIMIT = 60 * 1024 * 1024
 SLABS = 16
 COILS = 8
-BATCH = 2
+BATCH = 4
+RING = 4
 
 
 def kernel(image, cot, sens, labels, *rest):
@@ -335,13 +337,14 @@
     held = rest[len(WEIGHTS) + 1 : 2 * len(WEIGHTS) + 1]
     scratch = rest[2 * len(WEIGHTS) + 1 :]
     w = Refs(**dict(zip(WEIGHTS, held)), **dict(zip(WORK, scratch)))
-    (col, lab, piece, sens_all, own_cot, cot_all, line_parts, halo, final) = (
+    (col, lab, piece, sens_all, own_cot, cot_all, line_parts, halo, final, gathered) = (
         scratch[len(WORK) : len(WORK) + len(BUFFERS)]
     )
-    sems, sens_sem, ready = scratch[len(WORK) + len(BUFFERS) :]
+    sems, sens_sem, ag_sems, ready = scratch[len(WORK) + len(BUFFERS) :]
     (own_sem, field_sem, col_sem, cot_sem, line_sem, halo_sem, out_sem, send_sem, sens_send_sem) = [
         sems.at[i] for i in range(9)
     ]
+    y_sem, right_sem, left_sem, far_sem, right2_sem, left2_sem, far2_sem = [ag_sems.at[i] for i in range(7)]
     s = lax.axis_index("slab")
     c = lax.axis_index("coil")
     sends = []
@@ -403,15 +406,14 @@
         ).start()
 
     local(sens.at[:, :, :, lax.rem(16 * c + 8 + s, 128), :], sens_all.at[c, :, :, mine, :], sens_sem.at[c])
-    lax.fori_loop(1, SLABS, lambda d, carry: (send_line(lax.rem(s + d, SLABS), c), carry)[1], 0)
     pl.semaphore_wait(ready, SLABS - 1)
 
-    others = SLABS * (COILS - 1)
+    others = SLABS * COILS - 1
     share = EACH * HEADS * (TOKENS // CHUNK)
 
     def send_other(k):
-        d = lax.rem(STRIDE * k + 7, others)
-        send_line(lax.rem(s + lax.rem(d, SLABS), SLABS), lax.rem(c + 1 + d // SLABS, COILS))
+        d = lax.rem(STRIDE * k + 7, others) + 1
+        send_line(lax.rem(s + lax.rem(d, SLABS), SLABS), lax.rem(c + d // SLABS, COILS))
 
     for k in range(others - share * SENDING):
         send_other(k)
@@ -463,12 +465,45 @@
     final[:, 4:8] = final[:, 4:8] + piece[:, 0:4]
     await_bytes(halo, halo_sem)
     final[:, 0:4] = final[:, 0:4] + halo[...]
-    for d in range(1, COILS):
-        t = lax.rem(c + d, COILS)
-        for xs, place in zip(halves, places):
-            send(final.at[:, :, place, :], out.at[:, :, xs, :], out_sem, {"coil": t})
-    for xs, place in zip(halves, places):
-        local(final.at[:, :, place, :], out.at[:, :, xs, :], out_sem)
+    high = c // RING
+    across = lax.rem(c, RING)
+    right = RING * high + lax.rem(across + 1, RING)
+    left = RING * high + lax.rem(across + RING - 1, RING)
+    other = lax.rem(c + RING, COILS)
+
+    def column(coil, half):
+        return gathered.at[:, :, span(lax.rem(16 * coil + 8 + 8 * half, 128), 8, 8), :]
+
+    def pass_on(coil, half, target, sem):
+        block = column(coil, half)
+        send(block, block, sem, {"coil": target})
+
+    for half in range(2):
+        gathered[:, :, halves[half], :] = final[:, :, places[half], :]
+    for half in range(2):
+        pass_on(c, half, other, y_sem)
+    for half in (0, 1):
+        pass_on(c, half, right, right_sem)
+        pass_on(c, 1 - half, left, left_sem)
+    two = final.at[:, :, 0:16, :]
+    one = final.at[:, :, 0:8, :]
+    await_bytes(two, y_sem)
+    await_bytes(two, right_sem)
+    await_bytes(two, left_sem)
+    pass_on(left, 0, right, far_sem)
+    pass_on(right, 1, left, far_sem)
+    across_right = lax.rem(right + RING, COILS)
+    across_left = lax.rem(left + RING, COILS)
+    for half in (0, 1):
+        pass_on(other, half, right, right2_sem)
+        pass_on(other, 1 - half, left, left2_sem)
+    await_bytes(two, right2_sem)
+    await_bytes(two, left2_sem)
+    pass_on(across_left, 0, right, far2_sem)
+    pass_on(across_right, 1, left, far2_sem)
+    await_bytes(two, far_sem)
+    await_bytes(two, far2_sem)
+    local(gathered, out, out_sem)
     await_bytes(sens_all.at[0:7], sens_send_sem)
     await_bytes(sens_all.at[7, :, :, 0:120, :], sens_send_sem)
     await_bytes(out, out_sem)
@@ -484,6 +519,7 @@
     scratch += [
         pltpu.SemaphoreType.DMA((9,)),
         pltpu.SemaphoreType.DMA((COILS,)),
+        pltpu.SemaphoreType.DMA((7,)),
         pltpu.SemaphoreType.REGULAR,
     ]
     return pl.pallas_call(

time: 79.6 us -> 74.8 us (0.940)
  the two profiles are of different devices: /device:TPU:38 before, /device:TPU:0 now
where the time goes in v3:
time: 74.8 us; the launch traced here: 74.6 us
  Pallas kernels  72.3 us (97%)
  local copies, waits for them, and re-layouts  2.3 us (3%)
    pallas_call x1, Pallas kernels, body(): pl.pallas_call(kernel, out_shape=jax.ShapeDtypeStruct(image.shape, F32),...  72.3 us
    unnamed x1, local copies, waits for them, and re-layouts  2.3 us

profile of v3, /device:TPU:0, one launch (start us, length us, event | category | flops | bytes accessed | tf_op | source)
XLA Modules:
  0.0 74.6 jit_solution(2556867537667912569)
XLA Ops:
  0.0 72.3 %shard_map.127 = f32[2,8,128,128]{3,2,1,0:T(8,128)} custom-call(f32[2,8,128,128]{3,2,1,0:T(8,128)} %image.1, f32[2,8,128,128]{3,2,1,0:T(8,128)} %cot.1, f32[2,2,8,128,128]{4,3,2,1,0:T(8,128)} %sens.1, s32[8,64,64]{2,1,0:T(8,128)} %labels.1, s32[128,128]{1,0:T(8,128)} %rest_0_.1, f32[8,96]{1,0:T(8,128)} %rest_1_.1, f32[1,96]{1,0:T(1,128)} %bitcast.3, ...), custom_call_target="tpu_custom_call" | custom-call | tf_op jit(solution)/shard_map/pallas_call | solution.py:525
  72.3 2.3 %copy.15 = f32[2,8,128,128]{3,2,1,0:T(8,128)} copy(f32[2,8,128,128]{3,2,1,0:T(8,128)} %shard_map.127) | data formatting | bytes 2097152

commit v4 on v3

--- a/solution.py
+++ b/solution.py
@@ -478,6 +478,11 @@
         block = column(coil, half)
         send(block, block, sem, {"coil": target})
 
+    def keep(coil):
+        for half in range(2):
+            xs = span(lax.rem(16 * coil + 8 + 8 * half, 128), 8, 8)
+            local(gathered.at[:, :, xs, :], out.at[:, :, xs, :], out_sem)
+
     for half in range(2):
         gathered[:, :, halves[half], :] = final[:, :, places[half], :]
     for half in range(2):
@@ -497,13 +502,19 @@
     for half in (0, 1):
         pass_on(other, half, right, right2_sem)
         pass_on(other, 1 - half, left, left2_sem)
+    for coil in (c, other, right, left):
+        keep(coil)
     await_bytes(two, right2_sem)
     await_bytes(two, left2_sem)
     pass_on(across_left, 0, right, far2_sem)
     pass_on(across_right, 1, left, far2_sem)
+    keep(across_right)
+    keep(across_left)
+    far = RING * high + lax.rem(across + 2, RING)
     await_bytes(two, far_sem)
+    keep(far)
     await_bytes(two, far2_sem)
-    local(gathered, out, out_sem)
+    keep(lax.rem(far + RING, COILS))
     await_bytes(sens_all.at[0:7], sens_send_sem)
     await_bytes(sens_all.at[7, :, :, 0:120, :], sens_send_sem)
     await_bytes(out, out_sem)

time: 74.8 us -> 74.4 us (level)
  no operation moved by 1% of the time
where the time goes in v4:
time: 74.4 us; the launch traced here: 74.3 us
  Pallas kernels  72 us (97%)
  local copies, waits for them, and re-layouts  2.3 us (3%)
    pallas_call x1, Pallas kernels, body(): pl.pallas_call(kernel, out_shape=jax.ShapeDtypeStruct(image.shape, F32),...  72 us
    unnamed x1, local copies, waits for them, and re-layouts  2.3 us

profile of v4, /device:TPU:0, one launch (start us, length us, event | category | flops | bytes accessed | tf_op | source)
XLA Modules:
  0.0 74.3 jit_solution(10215423129557210759)
XLA Ops:
  0.0 72.0 %shard_map.127 = f32[2,8,128,128]{3,2,1,0:T(8,128)} custom-call(f32[2,8,128,128]{3,2,1,0:T(8,128)} %image.1, f32[2,8,128,128]{3,2,1,0:T(8,128)} %cot.1, f32[2,2,8,128,128]{4,3,2,1,0:T(8,128)} %sens.1, s32[8,64,64]{2,1,0:T(8,128)} %labels.1, s32[128,128]{1,0:T(8,128)} %rest_0_.1, f32[8,96]{1,0:T(8,128)} %rest_1_.1, f32[1,96]{1,0:T(1,128)} %bitcast.3, ...), custom_call_target="tpu_custom_call" | custom-call | tf_op jit(solution)/shard_map/pallas_call | solution.py:536
  72.0 2.3 %copy.15 = f32[2,8,128,128]{3,2,1,0:T(8,128)} copy(f32[2,8,128,128]{3,2,1,0:T(8,128)} %shard_map.127) | data formatting | bytes 2097152
